TPU v7x, 256 devices: a whole 4x4x8 slice. The times are simulated.
256 devices in a mesh: sect: 4 (over z_hi), ctx: 8 (over z_lo, y), tp: 8 (over x, core).
Axes of the slice: x: 4, y: 4, z: 8 (z_hi: 4, z_lo: 2; z = z_hi * 2 + z_lo), core: 2. Of those that a mesh axis runs over, the one named last changes fastest.
Arguments:
- patches: bfloat16 [4096, 1280], P(('sect', 'ctx')), may hold values from -6 to 6
- patch_gain: float32 [1280], replicated, may hold values from 0.25 to 1.75
- patch_shift: float32 [1280], replicated, may hold values from -3 to 3
- encoder_up: bfloat16 [1280, 5120], P(None, 'tp'), may hold values from -0.15625 to 0.15625
- encoder_down: bfloat16 [5120, 1280], P('tp'), may hold values from -0.078125 to 0.078125
- proj_weight: bfloat16 [1280, 8192], P(None, 'tp'), may hold values from -0.15625 to 0.15625
- hidden_text: bfloat16 [8192, 8192], P(('sect', 'ctx'), 'tp'), may hold values from -180 to 180
- slot_source: int32 [64], P(('sect', 'ctx')), may hold values from 0 to 4, as said below
- norm_gain: float32 [8192], P('tp'), may hold values from 0.25 to 1.75
- kv_weight: bfloat16 [2048, 8192], P(None, 'tp'), may hold values from -0.0625 to 0.0625
- queries: bfloat16 [8192, 4096], P(('sect', 'ctx'), 'tp'), may hold values from -40 to 40
Outputs:
- attended: bfloat16 [8192, 4096], P(('sect', 'ctx'), 'tp')
Inputs may be any that keep to these rules, and one draw needn't show every extreme that they name: `slot_source`: for each ctx index, the slots of the blocks with that index carry each value 0 to 3 exactly once, all other slots 4.
All inputs are finite; a program needn't handle non-finite values.
Results may differ from a plain program's by a relative error of at most 0.019.
Values may be sent and summed in bfloat16 or wider, within the bound.
No kernel may reach another device: no remote copies, remote signals or barrier semaphores. Data moves between devices by JAX's collectives and lax.ppermute only.
A program may use at most 128 MiB of HBM per device.

v0:
```python
from functools import partial
import math
import jax
import jax.numpy as jnp
from jax import lax
from jax.sharding import PartitionSpec as P

D = 8192
HEAD = 128
Q_HEADS = 32
KV_HEADS = 8
PATCHES = 128


def layer_norm(values, norm_scale, norm_shift):
    widened = values.astype(jnp.float32)
    center = jnp.mean(widened, axis=-1, keepdims=True)
    spread = jnp.mean(jnp.square(widened - center), axis=-1, keepdims=True)
    return ((widened - center) * lax.rsqrt(spread + 1e-06) * norm_scale + norm_shift).astype(
        jnp.bfloat16
    )


def rotate_keys(keys_in, positions):
    half_size = keys_in.shape[-2] // 2
    frequencies = jnp.exp(
        jnp.arange(half_size, dtype=jnp.float32) * (-2.0 * math.log(500000.0) / (2 * half_size))
    )
    angles = positions[None, :] * frequencies[:, None]
    cosine_table = jnp.cos(angles)
    sine_table = jnp.sin(angles)
    first_half = keys_in[..., :half_size, :]
    second_half = keys_in[..., half_size:, :]
    return jnp.concatenate(
        [
            first_half * cosine_table - second_half * sine_table,
            second_half * cosine_table + first_half * sine_table,
        ],
        axis=-2,
    )


def attend_update(state_now, queries_blk, query_pos, keys_blk, values_blk, key_pos):
    running_max, running_sum, accumulated = state_now
    scale_value = queries_blk.shape[-1] ** (-0.5)
    scores = (
        jnp.einsum("rkgd,kdn->kgrn", queries_blk, keys_blk, preferred_element_type=jnp.float32)
        * scale_value
    )
    allowed = query_pos[:, None] >= key_pos[None, :]
    scores = jnp.where(allowed, scores, -jnp.inf)
    new_max = jnp.maximum(running_max, jnp.max(scores, axis=-1))
    weights = jnp.exp(scores - new_max[..., None])
    running_sum = jnp.sum(weights, axis=-1)
    mixed_rows = jnp.einsum(
        "kgrn,kdn->kgrd",
        weights.astype(jnp.bfloat16),
        values_blk,
        preferred_element_type=jnp.float32,
    )
    accumulated = mixed_rows
    return (new_max, running_sum, accumulated)


def keep_state(state_now):
    return state_now


def fold_step(states, fragment, first_index, groups):
    key_tile, value_tile = fragment
    key_pos = jnp.arange(key_tile.shape[2], dtype=jnp.int32)
    updated = []
    for group_entry, state_now in zip(groups, states):
        group_queries, group_first = group_entry
        row_count = group_queries.shape[0]
        query_pos = group_first + jnp.arange(row_count, dtype=jnp.int32)
        runner = partial(
            attend_update,
            queries_blk=group_queries,
            query_pos=query_pos,
            keys_blk=key_tile,
            values_blk=value_tile,
            key_pos=key_pos,
        )
        updated.append(
            lax.cond(first_index <= group_first + row_count - 1, runner, keep_state, state_now)
        )
    return tuple(updated)


def initial_state(kv_count, group_size, row_count):
    return (
        jnp.full((kv_count, group_size, row_count), -1e30, jnp.float32),
        jnp.zeros((kv_count, group_size, row_count), jnp.float32),
        jnp.zeros((kv_count, group_size, row_count, HEAD), jnp.float32),
    )


def finish_state(state_now):
    final_max, final_sum, final_acc = state_now
    result = final_acc / final_sum[..., None]
    return jnp.transpose(result, (2, 0, 1, 3)).reshape(result.shape[2], -1).astype(jnp.bfloat16)


def body(
    patches,
    patch_gain,
    patch_shift,
    encoder_up,
    encoder_down,
    proj_weight,
    hidden_text,
    slot_source,
    norm_gain,
    kv_weight,
    queries,
):
    normed_patches = layer_norm(patches, patch_gain, patch_shift)
    enc_hidden = jax.nn.gelu(
        jnp.dot(normed_patches, encoder_up, preferred_element_type=jnp.float32), approximate=False
    ).astype(jnp.bfloat16)
    partial_out = jnp.dot(enc_hidden, encoder_down, preferred_element_type=jnp.float32)
    summed_out = lax.psum(partial_out, "tp")
    encoded = (patches.astype(jnp.float32) + summed_out).astype(jnp.bfloat16)
    image_emb = jnp.dot(encoded, proj_weight, preferred_element_type=jnp.float32).astype(
        jnp.bfloat16
    )
    slot_total = slot_source.shape[0]
    slots_start = hidden_text.reshape(slot_total, PATCHES, hidden_text.shape[1])
    current = slots_start
    fragment = lax.all_gather(image_emb, "sect", axis=0, tiled=True)
    first_source = jnp.int32(0) // PATCHES
    for offset in range(fragment.shape[0] // PATCHES):
        chosen = (slot_source == first_source + offset)[:, None, None]
        current = jnp.where(
            chosen, fragment[offset * PATCHES : (offset + 1) * PATCHES][None], current
        )
    merged = current.reshape(hidden_text.shape)
    widened = merged.astype(jnp.float32)
    square_sums = lax.psum(jnp.sum(jnp.square(widened), axis=1), "tp")
    inverse = lax.rsqrt(square_sums / D + 1e-05)
    normed_hidden = (widened * inverse[:, None] * norm_gain[None, :]).astype(jnp.bfloat16)
    head_rows = kv_weight.shape[0] // lax.axis_size("tp")
    projected = lax.psum_scatter(
        lax.dot_general(
            kv_weight, normed_hidden, (((1,), (1,)), ((), ())), preferred_element_type=jnp.float32
        ),
        "tp",
        scatter_dimension=0,
        tiled=True,
    )
    row_total = queries.shape[0]
    kv_count = head_rows // (2 * HEAD)
    projected = projected.reshape(kv_count, 2, HEAD, row_total)
    block_number = lax.axis_index(("sect", "ctx"))
    first_position = block_number * row_total
    positions = (first_position + jnp.arange(row_total, dtype=jnp.int32)).astype(jnp.float32)
    rotated = rotate_keys(projected[:, 0], positions).astype(jnp.bfloat16)
    value_rows = projected[:, 1].astype(jnp.bfloat16)
    group_size = Q_HEADS // KV_HEADS
    grouped_queries = queries.reshape(row_total, kv_count, group_size, HEAD)
    groups = ((grouped_queries, first_position),)
    initial = tuple(
        [initial_state(kv_count, group_size, group_entry[0].shape[0]) for group_entry in groups]
    )
    folder = partial(fold_step, groups=groups)
    finals = folder(
        initial,
        (
            lax.all_gather(rotated, ("sect", "ctx"), axis=2, tiled=True),
            lax.all_gather(value_rows, ("sect", "ctx"), axis=2, tiled=True),
        ),
        jnp.int32(0),
    )
    results = [finish_state(state_now) for state_now in finals]
    return results[0]


def solution(mesh):
    in_specs = (
        P(("sect", "ctx"), None),
        P(),
        P(),
        P(None, "tp"),
        P("tp", None),
        P(None, "tp"),
        P(("sect", "ctx"), "tp"),
        P(("sect", "ctx")),
        P("tp"),
        P(None, "tp"),
        P(("sect", "ctx"), "tp"),
    )
    out_specs = P(("sect", "ctx"), "tp")
    return jax.shard_map(body, mesh=mesh, in_specs=in_specs, out_specs=out_specs, check_vma=False)
```

profile of v0, /device:TPU:8, one launch (start us, length us, event | category | flops | bytes accessed | tf_op | source)
XLA Modules:
  0.0 383.6 jit_solution(16793101043001423742)
XLA Ops:
  6.5 0.0 copy-start
  6.5 0.0 all-reduce.2.cloned.1.call-start
  6.5 1.2 convert_reduce_fusion
  7.8 1.2 fusion.24
  9.0 0.0 copy-start.2
  9.0 4.4 %fusion.55 = f32[128,1280]{1,0:T(8,128)} fusion(bf16[640,1280]{1,0:T(8,128)(2,1)} %param.17, bf16[1280,640]{1,0:T(8,128)(2,1)} %param.16, bf16[128,1280]{1,0:T(8,128)(2,1)} %param.13, f32[1280]{0:T(1024)} %param.15, f32[1280]{0:T(1024)} %param.14, f32[128]{0:T(128)S(1)} %add_rsqrt_fusion.1, f32[128]{0:T(128)S(1)} %broadcast_multiply_fusion), kind=kOutput, calls=%fused_computation.67 | convolution fusion | flops 425738240 | bytes 4271104 | tf_op jit(solution)/shard_map/dot_general | solution.py:122
  13.4 0.0 copy-start.4
  13.4 0.0 copy-start.3
  13.4 0.0 all-reduce.2.cloned.1.call-update
  13.5 0.0 copy-start.6
  13.5 0.0 all-gather.5.cloned.1.call-start
  13.5 69.3 %all-reduce.2.cloned.1.call-done = f32[128,1280]{1,0:T(8,128)} async-done(((f32[128,1280]{1,0:T(8,128)}), f32[128,1280]{1,0:T(8,128)}) %all-reduce.2.cloned.1.call-update) | async-done | bytes 655376 | tf_op jit(solution)/shard_map/psum | solution.py:123
  82.8 0.0 copy-done
  82.8 0.0 copy-done.2
  82.9 2.3 convolution_convert_fusion
  85.2 0.0 all-gather.5.cloned.1.call-update
  85.2 0.0 reduce-scatter.2.cloned.1.call-start
  85.2 0.0 copy-done.4
  85.3 0.1 broadcast_bitcast_fusion.2
  85.3 0.1 broadcast_bitcast_fusion
  85.4 34.6 %all-gather.5.cloned.1.call-done = bf16[512,1024]{1,0:T(8,128)(2,1)} async-done(((bf16[128,1024]{1,0:T(8,128)(2,1)}), bf16[512,1024]{1,0:T(8,128)(2,1)}) %all-gather.5.cloned.1.call-update) | async-done | bytes 1048592 | tf_op jit(solution)/shard_map/all_gather | solution.py:131
  120.0 1.3 fusion.127
  121.3 0.0 copy-done.3
  121.3 1.6 fusion.19
  122.8 14.3 %psum.15 = f32[256]{0:T(256)S(1)} all-reduce(f32[256]{0:T(256)S(1)} %get-tuple-element.38), channel_id=1, replica_groups=mesh['sect'=4,'ctx'=8,'tp'=8] {'tp'}, use_global_device_ids=true, to_apply=%region_4.5 | all-reduce | flops 256 | bytes 2048 | tf_op jit(solution)/shard_map/psum | solution.py:140
  137.2 0.0 copy-done.6
  137.2 0.0 copy-start.5
  137.2 5.1 %convolution_bitcast_fusion = f32[2048,256]{0,1:T(8,128)} fusion(bf16[2048,1024]{1,0:T(8,128)(2,1)} %param.22, bf16[256,1024]{1,0:T(8,128)(2,1)} %get-tuple-element.39, f32[1024]{0:T(1024)S(1)} %copy-done.6, f32[256]{0:T(256)S(1)} %add_rsqrt_fusion), kind=kOutput, calls=%fused_computation.19 | convolution fusion | flops 1074790400 | bytes 6820864 | tf_op jit(solution)/shard_map/dot_general | solution.py:145
  142.3 0.0 reduce-scatter.2.cloned.1.call-update
  142.3 0.0 all-gather.7.cloned.1.call-start
  142.4 31.3 %reduce-scatter.2.cloned.1.call-done = f32[256,256]{0,1:T(8,128)} async-done(((f32[2048,256]{0,1:T(8,128)}), f32[256,256]{0,1:T(8,128)}) %reduce-scatter.2.cloned.1.call-update) | async-done | bytes 262160 | tf_op jit(solution)/shard_map/reduce_scatter | solution.py:144
  173.7 1.1 copy.20
  174.8 0.3 fusion.93
  175.1 0.6 pad_maximum_fusion
  175.7 0.0 all-gather.7.cloned.1.call-update
  175.8 0.2 all-gather.9.cloned.1.call-start
  176.0 0.6 slice.47
  176.6 0.0 all-gather.9.cloned.1.call-update
  176.6 73.0 %all-gather.7.cloned.1.call-done = bf16[1,128,8192]{2,1,0:T(8,128)(2,1)} async-done(((bf16[1,128,256]{2,1,0:T(8,128)(2,1)}), bf16[1,128,8192]{2,1,0:T(8,128)(2,1)}) %all-gather.7.cloned.1.call-update) | async-done | bytes 2097168 | tf_op jit(solution)/shard_map/all_gather | solution.py:170
  249.6 76.4 %all-gather.9.cloned.1.call-done = bf16[1,1,128,8192]{3,2,1,0:T(8,128)(2,1)} async-done(((bf16[1,1,128,256]{3,2,1,0:T(8,128)(2,1)}), bf16[1,1,128,8192]{3,2,1,0:T(8,128)(2,1)}) %all-gather.9.cloned.1.call-update) | async-done | bytes 2097168 | tf_op jit(solution)/shard_map/all_gather | solution.py:171
  326.1 0.0 copy-done.5
  326.1 49.8 %conditional.1 = (f32[1,4,256]{2,1,0:T(4,128)S(1)}, f32[1,4,256,128]{3,2,1,0:T(8,128)S(1)}) conditional(s32[]{:T(128)} %convert_element_type.65, () %tuple.13, (s32[]{:T(128)}, s32[256]{0:T(256)S(1)}, s32[8192]{0:T(1024)S(1)}, bf16[1,128,8192]{2,1,0:T(8,128)(2,1)}, bf16[256,512]{1,0:T(8,128)(2,1)S(1)}, ...), branch_computations={%region_6.7_spmd, %region_7.10_spmd} | conditional | flops 4389338112 | bytes 122481712 | solution.py:86
  326.1 3.7 broadcast_compare_fusion
  329.8 0.0 copy-start.1
  329.8 15.6 %fusion.2 = (f32[4,256]{1,0:T(4,128)S(1)}, f32[8192,256,4]{1,0,2:T(8,128)}) fusion(pred[256,8192]{0,1:T(8,128)(4,1)S(1)} %broadcast_compare_fusion, bf16[1,128,8192]{2,1,0:T(8,128)(2,1)} %get-tuple-element.35, bf16[256,512]{1,0:T(8,128)(2,1)S(1)} %get-tuple-element.31), kind=kOutput, calls=%fused_computation.4 | convolution fusion | flops 2172648448 | bytes 38014976 | tf_op jit(solution)/shard_map/cond/branch_1_fun/rkgd,kdn->kgrn/dot_general | solution.py:47
  345.5 0.0 copy-done.1
  345.5 15.8 %fusion.10 = f32[1,4,256,128]{3,2,1,0:T(8,128)S(1)} fusion(bf16[1,128,8192]{2,1,0:T(8,128)(2,1)} %get-tuple-element.25, f32[8192,256,4]{1,0,2:T(8,128)} %get-tuple-element.41, f32[4,256]{1,0:T(4,128)S(1)} %broadcast_maximum_fusion, pred[256,8192]{0,1:T(8,128)(4,1)} %copy-done.1), kind=kOutput, calls=%fused_computation.12 | convolution fusion | flops 2181038080 | bytes 38277120 | tf_op jit(solution)/shard_map/cond/branch_1_fun/kgrn,kdn->kgrd/dot_general | solution.py:55
  361.2 14.6 %fusion.1 = f32[4,256]{1,0:T(4,128)S(1)} fusion(f32[8192,256,4]{1,0,2:T(8,128)} %get-tuple-element.41, f32[4,256]{1,0:T(4,128)S(1)} %broadcast_maximum_fusion, pred[256,8192]{0,1:T(8,128)(4,1)} %copy-done.1), kind=kLoop, calls=%fused_computation.3 | loop fusion | flops 33553408 | bytes 35659776 | tf_op jit(solution)/shard_map/cond/branch_1_fun/reduce_sum | solution.py:54
  375.9 0.2 fusion.57
  376.1 0.2 copy.22
  376.3 0.7 copy.33
  (11 shorter events, 0.1 us)
Async XLA Ops:
  6.5 76.3 %copy-start = (bf16[1280,1024]{1,0:T(8,128)(2,1)S(1)}, bf16[1280,1024]{1,0:T(8,128)(2,1)}, u32[]{:S(2)}) copy-start(bf16[1280,1024]{1,0:T(8,128)(2,1)} %param.18) | copy-start | bytes 7864324
  6.5 76.3 %all-reduce.2.cloned.1.call-start = ((), (), s32[]{:S(2)}) async-start(), calls=%async_computation.1 | async-start | bytes 1310720 | tf_op jit(solution)/shard_map/psum | solution.py:123
  9.0 73.8 %copy-start.2 = (bf16[128,1280]{1,0:T(8,128)(2,1)S(1)}, bf16[128,1280]{1,0:T(8,128)(2,1)}, u32[]{:S(2)}) copy-start(bf16[128,1280]{1,0:T(8,128)(2,1)} %param.13) | copy-start | bytes 983044
  13.4 71.8 %copy-start.4 = (s32[2]{0:T(128)S(1)}, s32[2]{0:T(128)}, u32[]{:S(2)}) copy-start(s32[2]{0:T(128)} %param.20) | copy-start | bytes 28
  13.4 107.8 %copy-start.3 = (bf16[256,1024]{1,0:T(8,128)(2,1)S(1)}, bf16[256,1024]{1,0:T(8,128)(2,1)}, u32[]{:S(2)}) copy-start(bf16[256,1024]{1,0:T(8,128)(2,1)} %param.19) | copy-start | bytes 1572868
  13.5 123.7 %copy-start.6 = (f32[1024]{0:T(1024)S(1)}, f32[1024]{0:T(1024)}, u32[]{:S(2)}) copy-start(f32[1024]{0:T(1024)} %param.21) | copy-start | bytes 12292
  13.5 106.5 %all-gather.5.cloned.1.call-start = ((), (), s32[]{:S(2)}) async-start(), calls=%async_computation.2 | async-start | bytes 1310720 | tf_op jit(solution)/shard_map/all_gather | solution.py:131
  85.2 88.5 %reduce-scatter.2.cloned.1.call-start = ((), (), s32[]{:S(2)}) async-start(), calls=%async_computation.3 | async-start | bytes 2359296 | tf_op jit(solution)/shard_map/reduce_scatter | solution.py:144
  137.2 188.9 %copy-start.5 = (bf16[256,512]{1,0:T(8,128)(2,1)S(1)}, bf16[256,512]{1,0:T(8,128)(2,1)}, u32[]{:S(2)}) copy-start(bf16[256,512]{1,0:T(8,128)(2,1)} %param.23) | copy-start | bytes 786436
  142.3 107.3 %all-gather.7.cloned.1.call-start = ((), (), s32[]{:S(2)}) async-start(), calls=%async_computation.4 | async-start | bytes 2162688 | tf_op jit(solution)/shard_map/all_gather | solution.py:170
  175.8 150.3 %all-gather.9.cloned.1.call-start = ((), (), s32[]{:S(2)}) async-start(), calls=%async_computation.5 | async-start | bytes 2162688 | tf_op jit(solution)/shard_map/all_gather | solution.py:171
  329.8 15.6 %copy-start.1 = (pred[256,8192]{0,1:T(8,128)(4,1)}, pred[256,8192]{0,1:T(8,128)(4,1)S(1)}, u32[]{:S(2)}) copy-start(pred[256,8192]{0,1:T(8,128)(4,1)S(1)} %broadcast_compare_fusion) | copy-start | bytes 6291460 | tf_op jit(solution)/shard_map/cond
Sparse Core Ops, SparseCore 0:
  13.6 69.2 all-reduce.1
  85.3 34.6 all-gather.4
  142.4 31.1 reduce-scatter.1
  176.0 73.6 all-gather.6
  252.0 74.0 all-gather.8
where the time goes:
time: 384 us
  waiting for transfers between devices  285 us (74%)
  matrix products  43.2 us (11%)
  other arithmetic  23.6 us (6%)
  blocking collectives  14.3 us (4%)
  between operations  13.3 us (3%)
  local copies, waits for them, and re-layouts  4.12 us (1%)
    all_gather x1, waiting for transfers between devices, body(): lax.all_gather(value_rows, ('sect', 'ctx'), axis=2, tiled=True)  76.4 us
    all_gather x1, waiting for transfers between devices, body(): lax.all_gather(rotated, ('sect', 'ctx'), axis=2, tiled=True)  73 us
    psum x1, waiting for transfers between devices, body(): summed_out = lax.psum(partial_out, 'tp')  69.3 us
    all_gather x1, waiting for transfers between devices, body(): fragment = lax.all_gather(image_emb, 'sect', axis=0, tiled=True)  34.6 us
    reduce_scatter x1, waiting for transfers between devices, body(): lax.psum_scatter(lax.dot_general(kv_weight, normed_hidden, (((1,), (1,)),...  31.3 us
    dot_general x1, matrix products, attend_update(): jnp.einsum('kgrn,kdn->kgrd', weights.astype(jnp.bfloat16), values_blk, pr...  15.8 us
    dot_general x1, matrix products, attend_update(): jnp.einsum('rkgd,kdn->kgrn', queries_blk, keys_blk, preferred_element_typ...  15.6 us
    reduce_sum x1, other arithmetic, attend_update(): running_sum = jnp.sum(weights, axis=-1)  14.6 us
  transfers between devices with their start and end apart: 5, of which 5 were waited for; matrix products, arithmetic and copies ran while one was open for 0% of the time, Pallas kernels for 0%

commit v1 on v0

--- a/solution.py
+++ b/solution.py
@@ -1,3 +1,4 @@
+import functools
 from functools import partial
 import math
 import jax
@@ -10,6 +11,13 @@
 Q_HEADS = 32
 KV_HEADS = 8
 PATCHES = 128
+
+
+def extend_the_entries(own_rows, group_axis):
+    return lax.all_gather(own_rows, axis_name=group_axis).sum(axis=0)
+
+
+detail_node = functools.partial(extend_the_entries, group_axis="tp")
 
 
 def layer_norm(values, norm_scale, norm_shift):
@@ -137,7 +145,7 @@
         )
     merged = current.reshape(hidden_text.shape)
     widened = merged.astype(jnp.float32)
-    square_sums = lax.psum(jnp.sum(jnp.square(widened), axis=1), "tp")
+    square_sums = detail_node(jnp.sum(jnp.square(widened), axis=1))
     inverse = lax.rsqrt(square_sums / D + 1e-05)
     normed_hidden = (widened * inverse[:, None] * norm_gain[None, :]).astype(jnp.bfloat16)
     head_rows = kv_weight.shape[0] // lax.axis_size("tp")

time: 384 us -> 381 us (level)
    psum x1 -> x0, blocking collectives: 14.3 us -> none  [body(): square_sums = lax.psum(jnp.sum(jnp.square(widened), axis=1), 'tp')]
    all_gather x0 -> x1, blocking collectives: none -> 10.5 us  [extend_the_entries(): return lax.all_gather(own_rows, axis_name=group_axis).sum(axis=0)]
where the time goes in v1:
time: 381 us; the launch traced here: 380 us
  waiting for transfers between devices  285 us (75%)
  matrix products  43.2 us (11%)
  other arithmetic  23.7 us (6%)
  between operations  13.3 us (3%)
  blocking collectives  10.5 us (3%)
  local copies, waits for them, and re-layouts  4.13 us (1%)
    all_gather x1, waiting for transfers between devices, body(): lax.all_gather(value_rows, ('sect', 'ctx'), axis=2, tiled=True)  76.4 us
    all_gather x1, waiting for transfers between devices, body(): lax.all_gather(rotated, ('sect', 'ctx'), axis=2, tiled=True)  73.2 us
    psum x1, waiting for transfers between devices, body(): summed_out = lax.psum(partial_out, 'tp')  69.3 us
    all_gather x1, waiting for transfers between devices, body(): fragment = lax.all_gather(image_emb, 'sect', axis=0, tiled=True)  34.6 us
    reduce_scatter x1, waiting for transfers between devices, body(): lax.psum_scatter(lax.dot_general(kv_weight, normed_hidden, (((1,), (1,)),...  31.6 us
    dot_general x1, matrix products, attend_update(): jnp.einsum('kgrn,kdn->kgrd', weights.astype(jnp.bfloat16), values_blk, pr...  15.8 us
    dot_general x1, matrix products, attend_update(): jnp.einsum('rkgd,kdn->kgrn', queries_blk, keys_blk, preferred_element_typ...  15.6 us
    reduce_sum x1, other arithmetic, attend_update(): running_sum = jnp.sum(weights, axis=-1)  14.6 us
  transfers between devices with their start and end apart: 5, of which 5 were waited for; matrix products, arithmetic and copies ran while one was open for 0% of the time, Pallas kernels for 0%

profile of v1, /device:TPU:8, one launch (start us, length us, event | category | flops | bytes accessed | tf_op | source)
XLA Modules:
  0.0 380.3 jit_solution(5974026323606674378)
XLA Ops:
  6.5 0.0 copy-start
  6.5 0.0 all-reduce.2.cloned.1.call-start
  6.5 1.2 convert_reduce_fusion
  7.8 1.2 fusion.24
  9.0 0.0 copy-start.2
  9.0 4.4 %fusion.55 = f32[128,1280]{1,0:T(8,128)} fusion(bf16[640,1280]{1,0:T(8,128)(2,1)} %param.17, bf16[1280,640]{1,0:T(8,128)(2,1)} %param.16, bf16[128,1280]{1,0:T(8,128)(2,1)} %param.13, f32[1280]{0:T(1024)} %param.15, f32[1280]{0:T(1024)} %param.14, f32[128]{0:T(128)S(1)} %add_rsqrt_fusion.1, f32[128]{0:T(128)S(1)} %broadcast_multiply_fusion), kind=kOutput, calls=%fused_computation.67 | convolution fusion | flops 425738240 | bytes 4271104 | tf_op jit(solution)/shard_map/dot_general | solution.py:130
  13.4 0.0 copy-start.4
  13.4 0.0 copy-start.3
  13.4 0.0 all-reduce.2.cloned.1.call-update
  13.5 0.0 copy-start.6
  13.5 0.0 all-gather.7.cloned.1.call-start
  13.5 69.3 %all-reduce.2.cloned.1.call-done = f32[128,1280]{1,0:T(8,128)} async-done(((f32[128,1280]{1,0:T(8,128)}), f32[128,1280]{1,0:T(8,128)}) %all-reduce.2.cloned.1.call-update) | async-done | bytes 655376 | tf_op jit(solution)/shard_map/psum | solution.py:131
  82.8 0.0 copy-done
  82.8 0.0 copy-done.2
  82.9 2.3 convolution_convert_fusion
  85.2 0.0 all-gather.7.cloned.1.call-update
  85.2 0.0 reduce-scatter.2.cloned.1.call-start
  85.2 0.0 copy-done.4
  85.3 0.1 broadcast_bitcast_fusion.2
  85.3 0.1 broadcast_bitcast_fusion
  85.4 34.6 %all-gather.7.cloned.1.call-done = bf16[512,1024]{1,0:T(8,128)(2,1)} async-done(((bf16[128,1024]{1,0:T(8,128)(2,1)}), bf16[512,1024]{1,0:T(8,128)(2,1)}) %all-gather.7.cloned.1.call-update) | async-done | bytes 1048592 | tf_op jit(solution)/shard_map/all_gather | solution.py:139
  120.0 1.3 fusion.127
  121.3 0.0 copy-done.3
  121.3 1.6 fusion.19
  122.8 10.5 %all-gather.2 = f32[8,1,256]{2,1,0:T(1,128)S(1)} all-gather(f32[1,1,256]{2,1,0:T(1,128)S(1)} %bitcast.96), channel_id=2, replica_groups=mesh['sect'=4,'ctx'=8,'tp'=8] {'tp'}, dimensions={0}, use_global_device_ids=true | all-gather | bytes 9216 | tf_op jit(solution)/shard_map/all_gather | solution.py:17
  133.4 0.0 copy-done.6
  133.4 0.0 copy-start.5
  133.4 5.1 %convolution_bitcast_fusion = f32[2048,256]{0,1:T(8,128)} fusion(bf16[2048,1024]{1,0:T(8,128)(2,1)} %param.22, bf16[256,1024]{1,0:T(8,128)(2,1)} %get-tuple-element.39, f32[1024]{0:T(1024)S(1)} %copy-done.6, f32[256]{0:T(256)S(1)} %add_rsqrt_fusion), kind=kOutput, calls=%fused_computation.19 | convolution fusion | flops 1074790400 | bytes 6820864 | tf_op jit(solution)/shard_map/dot_general | solution.py:153
  138.4 0.0 reduce-scatter.2.cloned.1.call-update
  138.5 0.0 all-gather.9.cloned.1.call-start
  138.6 31.6 %reduce-scatter.2.cloned.1.call-done = f32[256,256]{0,1:T(8,128)} async-done(((f32[2048,256]{0,1:T(8,128)}), f32[256,256]{0,1:T(8,128)}) %reduce-scatter.2.cloned.1.call-update) | async-done | bytes 262160 | tf_op jit(solution)/shard_map/reduce_scatter | solution.py:152
  170.2 1.1 copy.25
  171.3 0.3 fusion.93
  171.6 0.6 pad_maximum_fusion
  172.2 0.0 all-gather.9.cloned.1.call-update
  172.3 0.2 all-gather.11.cloned.1.call-start
  172.5 0.6 slice.47
  173.1 0.0 all-gather.11.cloned.1.call-update
  173.1 73.2 %all-gather.9.cloned.1.call-done = bf16[1,128,8192]{2,1,0:T(8,128)(2,1)} async-done(((bf16[1,128,256]{2,1,0:T(8,128)(2,1)}), bf16[1,128,8192]{2,1,0:T(8,128)(2,1)}) %all-gather.9.cloned.1.call-update) | async-done | bytes 2097168 | tf_op jit(solution)/shard_map/all_gather | solution.py:178
  246.3 76.4 %all-gather.11.cloned.1.call-done = bf16[1,1,128,8192]{3,2,1,0:T(8,128)(2,1)} async-done(((bf16[1,1,128,256]{3,2,1,0:T(8,128)(2,1)}), bf16[1,1,128,8192]{3,2,1,0:T(8,128)(2,1)}) %all-gather.11.cloned.1.call-update) | async-done | bytes 2097168 | tf_op jit(solution)/shard_map/all_gather | solution.py:179
  322.7 0.0 copy-done.5
  322.7 49.8 %conditional.1 = (f32[1,4,256]{2,1,0:T(4,128)S(1)}, f32[1,4,256,128]{3,2,1,0:T(8,128)S(1)}) conditional(s32[]{:T(128)} %convert_element_type.65, () %tuple.13, (s32[]{:T(128)}, s32[256]{0:T(256)S(1)}, s32[8192]{0:T(1024)S(1)}, bf16[1,128,8192]{2,1,0:T(8,128)(2,1)}, bf16[256,512]{1,0:T(8,128)(2,1)S(1)}, ...), branch_computations={%region_6.7_spmd, %region_7.10_spmd} | conditional | flops 4389338112 | bytes 122481712 | solution.py:94
  322.7 3.7 broadcast_compare_fusion
  326.5 0.0 copy-start.1
  326.5 15.6 %fusion.2 = (f32[4,256]{1,0:T(4,128)S(1)}, f32[8192,256,4]{1,0,2:T(8,128)}) fusion(pred[256,8192]{0,1:T(8,128)(4,1)S(1)} %broadcast_compare_fusion, bf16[1,128,8192]{2,1,0:T(8,128)(2,1)} %get-tuple-element.35, bf16[256,512]{1,0:T(8,128)(2,1)S(1)} %get-tuple-element.31), kind=kOutput, calls=%fused_computation.4 | convolution fusion | flops 2172648448 | bytes 38014976 | tf_op jit(solution)/shard_map/cond/branch_1_fun/rkgd,kdn->kgrn/dot_general | solution.py:55
  342.1 0.0 copy-done.1
  342.1 15.8 %fusion.10 = f32[1,4,256,128]{3,2,1,0:T(8,128)S(1)} fusion(bf16[1,128,8192]{2,1,0:T(8,128)(2,1)} %get-tuple-element.25, f32[8192,256,4]{1,0,2:T(8,128)} %get-tuple-element.41, f32[4,256]{1,0:T(4,128)S(1)} %broadcast_maximum_fusion, pred[256,8192]{0,1:T(8,128)(4,1)} %copy-done.1), kind=kOutput, calls=%fused_computation.12 | convolution fusion | flops 2181038080 | bytes 38277120 | tf_op jit(solution)/shard_map/cond/branch_1_fun/kgrn,kdn->kgrd/dot_general | solution.py:63
  357.9 14.6 %fusion.1 = f32[4,256]{1,0:T(4,128)S(1)} fusion(f32[8192,256,4]{1,0,2:T(8,128)} %get-tuple-element.41, f32[4,256]{1,0:T(4,128)S(1)} %broadcast_maximum_fusion, pred[256,8192]{0,1:T(8,128)(4,1)} %copy-done.1), kind=kLoop, calls=%fused_computation.3 | loop fusion | flops 33553408 | bytes 35659776 | tf_op jit(solution)/shard_map/cond/branch_1_fun/reduce_sum | solution.py:62
  372.6 0.2 fusion.57
  372.8 0.2 copy.27
  373.0 0.7 copy.38
  (12 shorter events, 0.1 us)
Async XLA Ops:
  6.5 76.3 %copy-start = (bf16[1280,1024]{1,0:T(8,128)(2,1)S(1)}, bf16[1280,1024]{1,0:T(8,128)(2,1)}, u32[]{:S(2)}) copy-start(bf16[1280,1024]{1,0:T(8,128)(2,1)} %param.18) | copy-start | bytes 7864324
  6.5 76.3 %all-reduce.2.cloned.1.call-start = ((), (), s32[]{:S(2)}) async-start(), calls=%async_computation.1 | async-start | bytes 1310720 | tf_op jit(solution)/shard_map/psum | solution.py:131
  9.0 73.8 %copy-start.2 = (bf16[128,1280]{1,0:T(8,128)(2,1)S(1)}, bf16[128,1280]{1,0:T(8,128)(2,1)}, u32[]{:S(2)}) copy-start(bf16[128,1280]{1,0:T(8,128)(2,1)} %param.13) | copy-start | bytes 983044
  13.4 71.8 %copy-start.4 = (s32[2]{0:T(128)S(1)}, s32[2]{0:T(128)}, u32[]{:S(2)}) copy-start(s32[2]{0:T(128)} %param.20) | copy-start | bytes 28
  13.4 107.8 %copy-start.3 = (bf16[256,1024]{1,0:T(8,128)(2,1)S(1)}, bf16[256,1024]{1,0:T(8,128)(2,1)}, u32[]{:S(2)}) copy-start(bf16[256,1024]{1,0:T(8,128)(2,1)} %param.19) | copy-start | bytes 1572868
  13.5 119.9 %copy-start.6 = (f32[1024]{0:T(1024)S(1)}, f32[1024]{0:T(1024)}, u32[]{:S(2)}) copy-start(f32[1024]{0:T(1024)} %param.21) | copy-start | bytes 12292
  13.5 106.5 %all-gather.7.cloned.1.call-start = ((), (), s32[]{:S(2)}) async-start(), calls=%async_computation.2 | async-start | bytes 1310720 | tf_op jit(solution)/shard_map/all_gather | solution.py:139
  85.2 85.0 %reduce-scatter.2.cloned.1.call-start = ((), (), s32[]{:S(2)}) async-start(), calls=%async_computation.3 | async-start | bytes 2359296 | tf_op jit(solution)/shard_map/reduce_scatter | solution.py:152
  133.4 189.4 %copy-start.5 = (bf16[256,512]{1,0:T(8,128)(2,1)S(1)}, bf16[256,512]{1,0:T(8,128)(2,1)}, u32[]{:S(2)}) copy-start(bf16[256,512]{1,0:T(8,128)(2,1)} %param.23) | copy-start | bytes 786436
  138.5 107.8 %all-gather.9.cloned.1.call-start = ((), (), s32[]{:S(2)}) async-start(), calls=%async_computation.4 | async-start | bytes 2162688 | tf_op jit(solution)/shard_map/all_gather | solution.py:178
  172.3 150.4 %all-gather.11.cloned.1.call-start = ((), (), s32[]{:S(2)}) async-start(), calls=%async_computation.5 | async-start | bytes 2162688 | tf_op jit(solution)/shard_map/all_gather | solution.py:179
  326.5 15.6 %copy-start.1 = (pred[256,8192]{0,1:T(8,128)(4,1)}, pred[256,8192]{0,1:T(8,128)(4,1)S(1)}, u32[]{:S(2)}) copy-start(pred[256,8192]{0,1:T(8,128)(4,1)S(1)} %broadcast_compare_fusion) | copy-start | bytes 6291460 | tf_op jit(solution)/shard_map/cond
Sparse Core Ops, SparseCore 0:
  13.6 69.2 all-reduce.1
  85.3 34.6 all-gather.6
  138.6 31.5 reduce-scatter.1
  172.5 73.7 all-gather.8
  248.6 74.0 all-gather.10
